TPU v7x, 32 devices: a whole 2x2x4 slice. The times are simulated.
32 devices in a mesh: ex: 4 (over y, x), pb: 8 (over z, core).
Axes of the slice: x: 2, y: 2, z: 4, core: 2. Of those that a mesh axis runs over, the one named last changes fastest.
Arguments:
- train_features: bfloat16 [32768, 4096], P('ex', 'pb'), may hold values from -6 to 6
- query_features: bfloat16 [2048, 4096], P('ex', 'pb'), may hold values from -6 to 6
- precond: bfloat16 [4096, 4096], P('pb'), may hold values from -0.09375 to 0.09375
- example_weight: float32 [32768], P(('ex', 'pb')), may hold values from 0.05 to 0.95
- select: int32 [16, 256], P(None, ('ex', 'pb')), may hold values from 0 to 1, as said below
Outputs:
- scores: float32 [2048, 32768], P(None, ('ex', 'pb'))
Inputs may be any that keep to these rules, and one draw needn't show every extreme that they name: `select`: 1 where the pair of query block and training block is to be scored, else 0; the number of listed pairs differs widely between query blocks and between training blocks.
All inputs are finite; a program needn't handle non-finite values.
Results may differ from a plain program's by a relative error of at most 0.0029.
Values may be sent and summed in bfloat16 or wider, within the bound.
A program may use at most 128 MiB of HBM per device.

v0:
```python
import jax
import jax.numpy as jnp
from jax import lax
from jax.sharding import PartitionSpec as P

BLK = 128


def tile_product(portion, train_tile):
    return lax.dot_general(
        portion, train_tile, (((1,), (1,)), ((), ())), preferred_element_type=jnp.float32
    )


def on_device(train_features, query_features, precond, example_weight, select):
    rows_here = lax.all_to_all(train_features, "pb", split_axis=0, concat_axis=1, tiled=True)
    feature_width = rows_here.shape[1]
    summed = lax.psum_scatter(
        jnp.dot(query_features, precond, preferred_element_type=jnp.float32),
        "pb",
        scatter_dimension=0,
        tiled=True,
    )
    gathered = lax.all_gather(summed.astype(jnp.bfloat16), "pb", axis=0, tiled=True)
    block_count = select.shape[0]
    train_blocks = select.shape[1]
    product_part = tile_product(lax.all_gather(gathered, "ex", axis=0, tiled=True), rows_here)
    scaled = product_part * feature_width ** (-0.5) * example_weight[None, :]
    keep_mask = select.astype(jnp.float32)
    masked = scaled.reshape(block_count, BLK, train_blocks, BLK) * keep_mask[:, None, :, None]
    return masked.reshape(product_part.shape)


def solution(mesh):
    placed = (P("ex", "pb"), P("ex", "pb"), P("pb", None), P(("ex", "pb")), P(None, ("ex", "pb")))
    return jax.shard_map(
        on_device, mesh=mesh, in_specs=placed, out_specs=P(None, ("ex", "pb")), check_vma=False
    )
```

profile of v0, /device:TPU:0, one launch (start us, length us, event | category | flops | bytes accessed | tf_op | source)
XLA Modules:
  0.0 388.4 jit_solution(2467015767967976126)
XLA Ops:
  6.5 0.0 copy-start
  6.5 0.0 reduce-scatter.2.cloned.1.call-start
  6.5 1.0 copy-done
  7.6 7.9 %fusion = f32[512,4096]{1,0:T(8,128)} fusion(bf16[512,512]{1,0:T(8,128)(2,1)S(1)} %copy-done, bf16[512,4096]{1,0:T(8,128)(2,1)} %param.7), kind=kOutput, calls=%fused_computation.2 | convolution fusion | flops 2147483648 | bytes 13107200 | tf_op jit(solution)/shard_map/dot_general | solution.py:19
  15.5 0.0 reduce-scatter.2.cloned.1.call-update
  15.5 0.0 all-gather.3.cloned.1.call-start
  15.6 92.4 %reduce-scatter.2.cloned.1.call-done = f32[64,4096]{1,0:T(8,128)} async-done(((f32[512,4096]{1,0:T(8,128)}), f32[64,4096]{1,0:T(8,128)}) %reduce-scatter.2.cloned.1.call-update) | async-done | bytes 1048592 | tf_op jit(solution)/shard_map/reduce_scatter | solution.py:18
  108.0 2.1 convert_element_type.6
  110.1 0.0 all-gather.3.cloned.1.call-update
  110.1 0.0 all-gather.5.cloned.1.call-start
  110.2 45.6 %all-gather.3.cloned.1.call-done = bf16[512,4096]{1,0:T(8,128)(2,1)} async-done(((bf16[64,4096]{1,0:T(8,128)(2,1)}), bf16[512,4096]{1,0:T(8,128)(2,1)}) %all-gather.3.cloned.1.call-update) | async-done | bytes 4194320 | tf_op jit(solution)/shard_map/all_gather | solution.py:24
  155.7 0.0 all-gather.5.cloned.1.call-update
  155.8 0.0 copy-start.3
  155.8 0.0 copy-start.4
  155.8 5.0 %all-to-all-start = ((bf16[8,1024,512]{2,1,0:T(8,128)(2,1)}), bf16[8,1024,512]{2,1,0:T(8,128)(2,1)}, u32[]{:S(2)}, u32[]{:S(2)}) async-start(bf16[8,1024,512]{2,1,0:T(8,128)(2,1)} %bitcast.12), calls=%async_computation.1 | async-start | bytes 16777216 | tf_op jit(solution)/shard_map/all_to_all | solution.py:16
  160.8 0.0 copy-done.3
  160.8 0.1 copy.9
  160.9 0.0 copy-done.4
  160.9 183.8 %all-to-all-done = bf16[8,1024,512]{2,1,0:T(8,128)(2,1)} async-done(((bf16[8,1024,512]{2,1,0:T(8,128)(2,1)}), bf16[8,1024,512]{2,1,0:T(8,128)(2,1)}, u32[]{:S(2)}, u32[]{:S(2)}) %all-to-all-start) | async-done | bytes 8388640 | tf_op jit(solution)/shard_map/all_to_all | solution.py:16
  344.6 11.4 %copy.8 = bf16[1024,8,512]{0,2,1:T(8,128)(2,1)} copy(bf16[1024,8,512]{2,0,1:T(8,128)(2,1)} %bitcast.1) | data formatting | bytes 16777216 | tf_op jit(solution)/shard_map/all_to_all | solution.py:16
  356.0 0.0 all-gather.5.cloned.1.call-done
  356.0 0.0 copy-start.2
  356.0 0.6 mul.29
  356.6 2.8 copy-done.2
  359.4 0.0 copy-start.1
  359.4 22.5 %bitcast_multiply_fusion = f32[2048,1024]{1,0:T(8,128)} fusion(f32[256,8,8,128]{3,2,1,0:T(8,128)S(1)} %bitcast.11, bf16[2048,4096]{1,0:T(8,128)(2,1)} %all-gather.5.cloned.1.call-done, bf16[1024,4096]{0,1:T(8,128)(2,1)S(1)} %bitcast.13, f32[1024]{0:T(1024)S(1)} %broadcast_multiply_fusion), kind=kOutput, calls=%fused_computation | convolution fusion | flops 17184063488 | bytes 41947136 | tf_op jit(solution)/shard_map/dot_general | solution.py:10
  381.9 0.0 copy-done.1
  (2 shorter events, 0.0 us)
Async XLA Ops:
  6.5 1.0 copy-start
  6.5 101.5 %reduce-scatter.2.cloned.1.call-start = ((), (), s32[]{:S(2)}) async-start(), calls=%async_computation.2 | async-start | bytes 9437184 | tf_op jit(solution)/shard_map/reduce_scatter | solution.py:18
  15.5 140.2 %all-gather.3.cloned.1.call-start = ((), (), s32[]{:S(2)}) async-start(), calls=%async_computation.3 | async-start | bytes 4718592 | tf_op jit(solution)/shard_map/all_gather | solution.py:24
  110.1 245.9 %all-gather.5.cloned.1.call-start = ((), (), s32[]{:S(2)}) async-start(), calls=%async_computation.4 | async-start | bytes 20971520 | tf_op jit(solution)/shard_map/all_gather | solution.py:27
  155.8 5.0 %copy-start.3 = (s32[16,8]{0,1:T(8,128)S(1)}, s32[16,8]{0,1:T(8,128)}, u32[]{:S(2)}) copy-start(s32[16,8]{0,1:T(8,128)} %param.9) | copy-start | bytes 1540
  155.8 5.1 %copy-start.4 = (f32[1024]{0:T(1024)S(1)}, f32[1024]{0:T(1024)}, u32[]{:S(2)}) copy-start(f32[1024]{0:T(1024)} %param.8) | copy-start | bytes 12292
  155.8 188.9 %all-to-all-start = ((bf16[8,1024,512]{2,1,0:T(8,128)(2,1)}), bf16[8,1024,512]{2,1,0:T(8,128)(2,1)}, u32[]{:S(2)}, u32[]{:S(2)}) async-start(bf16[8,1024,512]{2,1,0:T(8,128)(2,1)} %bitcast.12), calls=%async_computation.1 | async-start | bytes 16777216 | tf_op jit(solution)/shard_map/all_to_all | solution.py:16
  356.0 3.4 copy-start.2
  359.4 22.5 %copy-start.1 = (bf16[512,512]{1,0:T(8,128)(2,1)S(1)}, bf16[512,512]{1,0:T(8,128)(2,1)}, u32[]{:S(2)}) copy-start(bf16[512,512]{1,0:T(8,128)(2,1)} %param.6) | copy-start | bytes 1572868
Sparse Core Ops, SparseCore 0:
  15.7 92.3 reduce-scatter.1
  110.2 45.4 all-gather.2
  157.6 156.1 all-gather.4
where the time goes:
time: 389 us; the launch traced here: 388 us
  waiting for transfers between devices  322 us (83%)
  matrix products  30.4 us (8%)
  local copies, waits for them, and re-layouts  15.9 us (4%)
  between operations  13.2 us (3%)
  starting transfers between devices  5.05 us (1%)
    all_to_all x1, waiting for transfers between devices, on_device(): lax.all_to_all(train_features, 'pb', split_axis=0, concat_axis=1, tiled=T...  184 us
    reduce_scatter x1, waiting for transfers between devices, on_device(): lax.psum_scatter(jnp.dot(query_features, precond, preferred_element_type=...  92.4 us
    all_gather x1, waiting for transfers between devices, on_device(): lax.all_gather(summed.astype(jnp.bfloat16), 'pb', axis=0, tiled=True)  45.6 us
    dot_general x1, matrix products, tile_product(): lax.dot_general(portion, train_tile, (((1,), (1,)), ((), ())), preferred_...  22.5 us
    all_to_all x1, local copies, waits for them, and re-layouts, on_device(): lax.all_to_all(train_features, 'pb', split_axis=0, concat_axis=1, tiled=T...  11.4 us
    dot_general x1, matrix products, on_device(): jnp.dot(query_features, precond, preferred_element_type=jnp.float32)  7.93 us
  transfers between devices with their start and end apart: 4, of which 3 were waited for; matrix products, arithmetic and copies ran while one was open for 3% of the time, Pallas kernels for 0%

commit v1 on v0

v1 whole, which is shorter than its diff:
```python
import functools

import jax
import jax.numpy as jnp
from jax import lax
from jax.experimental import pallas as pl
from jax.experimental.pallas import tpu as pltpu
from jax.sharding import PartitionSpec as P

BLK = 128
ROW_TILE = 512


def flip(index, mask):
    bit = 1
    while bit <= mask:
        if mask & bit:
            index = index + bit * (1 - 2 * ((index // bit) % 2))
        bit *= 2
    return index


def bits_of(count):
    return [1 << position for position in range(count.bit_length() - 1)]


def gather_stages(order):
    held, stages = [0], []
    for bit in order:
        stages.append((bit, list(held)))
        held = held + [mask ^ bit for mask in held]
    return stages


def copy_count(ex_count, pb_count):
    return 8 * pb_count + 8 * ex_count


def kernel(ex_count, pb_count, train, query, pre, out, q_all, p_all, c_all, t_all, c_sum, send_sem, recv_sem, local_sem):
    e, p = lax.axis_index("ex"), lax.axis_index("pb")
    core, line = p % 2, p // 2
    rows, width = query.shape
    share = pre.shape[0] // ex_count
    t_rows = t_all.shape[1]
    pb_bits, ex_bits = bits_of(pb_count), bits_of(ex_count)
    top = pb_bits[-1]

    barrier = pltpu.get_barrier_semaphore()
    for mask in range(1, pb_count):
        pl.semaphore_signal(barrier, inc=1, device_id={"pb": flip(p, mask)}, device_id_type=pl.DeviceIdType.MESH)
    for bit in ex_bits:
        pl.semaphore_signal(barrier, inc=1, device_id={"ex": flip(e, bit)}, device_id_type=pl.DeviceIdType.MESH)
    pl.semaphore_wait(barrier, pb_count - 1 + len(ex_bits))

    used = []

    def send(source, target, device):
        number = len(used)
        copy = pltpu.make_async_remote_copy(
            src_ref=source,
            dst_ref=target,
            send_sem=send_sem.at[number],
            recv_sem=recv_sem.at[number],
            device_id=device,
            device_id_type=pl.DeviceIdType.MESH,
        )
        copy.start()
        used.append(copy)
        return copy

    def arrive(copies):
        for copy in copies:
            copy.wait_recv()

    def own(source, target, number):
        copy = pltpu.make_async_copy(source, target, local_sem.at[number])
        copy.start()
        return copy

    def start_train(mask):
        owner = flip(p, mask)
        block = train.at[pl.ds(pl.multiple_of(owner * t_rows, t_rows), t_rows), :]
        return send(block, t_all.at[p], {"pb": owner})

    def start_query(stage):
        bit, held = stage
        copies = []
        for mask in held:
            where = flip(p, mask)
            source = query if mask == 0 else q_all.at[where]
            copies.append(send(source, q_all.at[where], {"pb": flip(p, bit)}))
        return copies

    def pre_part(owner):
        return pre.at[
            pl.ds(pl.multiple_of(e * share, share), share),
            pl.ds(pl.multiple_of(owner * width, width), width),
        ]

    query_stages = gather_stages(pb_bits[::-1])
    pending_q = start_query(query_stages[0])
    pending_p = []
    for mask in range(pb_count - 1, 0, -1):
        owner = flip(p, mask)
        pending_p.append(send(pre_part(owner), p_all.at[p, e], {"pb": owner}))
    local = [
        own(query, q_all.at[p], 0),
        own(pre_part(p), p_all.at[p, e], 1),
        own(train.at[pl.ds(pl.multiple_of(p * t_rows, t_rows), t_rows), :], t_all.at[p], 2),
    ]
    far = list(range(pb_count - 1, top - 1, -1))
    near = list(range(top - 1, 0, -1))
    train_copies = {}
    early = far[: len(far) // 2]
    for mask in early[:1]:
        train_copies[mask] = start_train(mask)
    local[0].wait()
    local[1].wait()
    arrive(pending_q)
    pending_q = start_query(query_stages[1])
    arrive(pending_p)

    half = pb_count // 2
    ex_orders = [ex_bits, ex_bits[1:] + ex_bits[:1]]
    ex_stages = [gather_stages(order) for order in ex_orders]

    q_next = 2
    for step in range(len(ex_bits)):
        pending = []
        for side in range(2):
            bit, held = ex_stages[side][step]
            for mask in held:
                part = p_all.at[pl.ds(side * half, half), flip(e, mask)]
                pending.append(send(part, part, {"ex": flip(e, bit)}))
        if q_next < len(query_stages):
            arrive(pending_q)
            pending_q = start_query(query_stages[q_next])
            q_next += 1
        arrive(pending)
    while q_next < len(query_stages):
        arrive(pending_q)
        pending_q = start_query(query_stages[q_next])
        q_next += 1
    arrive(pending_q)
    for mask in early[1:]:
        train_copies[mask] = start_train(mask)

    c_sum[...] = jnp.zeros_like(c_sum)

    def accumulate(block, carry):
        c_sum[...] += jnp.dot(
            q_all[block],
            p_all[block].reshape(ex_count * share, width),
            preferred_element_type=jnp.float32,
        )
        return carry

    lax.fori_loop(0, pb_count, accumulate, 0)
    own_rows = pl.ds(pl.multiple_of(e * rows, rows), rows)
    c_all[core, line, own_rows, :] = c_sum[...].astype(jnp.bfloat16)

    across = {"pb": flip(p, 1)}
    handed = []
    for bit, held in gather_stages([bit // 2 for bit in pb_bits[:0:-1]]):
        pending = []
        for mask in held:
            part = c_all.at[core, flip(line, mask), own_rows, :]
            pending.append(send(part, part, {"pb": flip(p, 2 * bit)}))
        arrive(pending)
    for mask in far:
        if mask not in train_copies:
            train_copies[mask] = start_train(mask)
    part = c_all.at[core, :, own_rows, :]
    handed.append(send(part, part, across))
    for mask in near:
        train_copies[mask] = start_train(mask)
    side_rows = rows // 2
    for step in range(len(ex_bits)):
        pending, arriving = [], []
        for side in range(2):
            bit, held = ex_stages[side][step]
            for mask in held:
                first = flip(e, mask) * rows + side * side_rows
                part = c_all.at[core, :, pl.ds(pl.multiple_of(first, side_rows), side_rows), :]
                pending.append(send(part, part, {"ex": flip(e, bit)}))
                first = flip(e, mask ^ bit) * rows + side * side_rows
                arriving.append(c_all.at[core, :, pl.ds(pl.multiple_of(first, side_rows), side_rows), :])
        for copy, part in zip(pending, arriving):
            copy.wait_recv()
            handed.append(send(part, part, across))
    arrive(handed)

    for mask in range(pb_count):
        if mask == 0:
            local[2].wait()
        else:
            train_copies[mask].wait_recv()
        block = flip(p, mask)

        def tile(step, carry, block=block, mask=mask):
            at = pl.ds(pl.multiple_of(step * ROW_TILE, ROW_TILE), ROW_TILE)
            product = lax.dot_general(
                c_all[block % 2, block // 2, at, :],
                t_all[block],
                (((1,), (1,)), ((), ())),
                preferred_element_type=jnp.float32,
            )
            if mask == 0:
                out[at, :] = product
            else:
                out[at, :] += product
            return carry

        lax.fori_loop(0, out.shape[0] // ROW_TILE, tile, 0)

    for copy in used:
        copy.wait_send()


def on_device(ex_count, pb_count, train_features, query_features, precond, example_weight, select):
    rows, width = query_features.shape
    t_rows = train_features.shape[0] // pb_count
    queries = rows * ex_count
    share = precond.shape[0] // ex_count
    feature_width = width * pb_count
    copies = copy_count(ex_count, pb_count)
    raw = pl.pallas_call(
        functools.partial(kernel, ex_count, pb_count),
        out_shape=jax.ShapeDtypeStruct((queries, t_rows), jnp.float32),
        in_specs=[pl.BlockSpec(memory_space=pl.ANY)] * 3,
        out_specs=pl.BlockSpec(memory_space=pltpu.VMEM),
        scratch_shapes=[
            pltpu.VMEM((pb_count, rows, width), jnp.bfloat16),
            pltpu.VMEM((pb_count, ex_count, share, width), jnp.bfloat16),
            pltpu.VMEM((2, pb_count // 2, queries, width), jnp.bfloat16),
            pltpu.VMEM((pb_count, t_rows, width), jnp.bfloat16),
            pltpu.VMEM((rows, width), jnp.float32),
            pltpu.SemaphoreType.DMA((copies,)),
            pltpu.SemaphoreType.DMA((copies,)),
            pltpu.SemaphoreType.DMA((3,)),
        ],
        compiler_params=pltpu.CompilerParams(
            collective_id=0, has_side_effects=True, vmem_limit_bytes=56 * 1024 * 1024
        ),
    )(train_features, query_features, precond)
    scaled = raw * feature_width ** (-0.5) * example_weight[None, :]
    keep_mask = select.astype(jnp.float32)
    masked = scaled.reshape(select.shape[0], BLK, select.shape[1], BLK) * keep_mask[:, None, :, None]
    return masked.reshape(raw.shape)


def solution(mesh):
    placed = (P("ex", "pb"), P("ex", "pb"), P("pb", None), P(("ex", "pb")), P(None, ("ex", "pb")))
    return jax.shard_map(
        functools.partial(on_device, mesh.shape["ex"], mesh.shape["pb"]),
        mesh=mesh,
        in_specs=placed,
        out_specs=P(None, ("ex", "pb")),
        check_vma=False,
    )
```

time: 389 us -> 332 us (0.85)
  waiting for transfers between devices: 322 us -> 0 us
  Pallas kernels: 0 us -> 314 us
  matrix products: 30.4 us -> 0 us
  between operations: 13.2 us -> 0.01 us
  local copies, waits for them, and re-layouts: 15.9 us -> 3.9 us
  other arithmetic: 2.08 us -> 13.7 us
  starting transfers between devices: 5.05 us -> 0 us
    pallas_call x0 -> x1, Pallas kernels: none -> 314 us  [on_device(): pl.pallas_call(functools.partial(kernel, ex_count, pb_count), out_shape=j...]
    all_to_all x1 -> x0, waiting for transfers between devices: 184 us -> none  [on_device(): lax.all_to_all(train_features, 'pb', split_axis=0, concat_axis=1, tiled=T...]
    reduce_scatter x1 -> x0, waiting for transfers between devices: 92.4 us -> none  [on_device(): lax.psum_scatter(jnp.dot(query_features, precond, preferred_element_type=...]
    all_gather x2 -> x0, waiting for transfers between devices: 45.6 us -> none  [the longest x1 45.6 us: on_device(): lax.all_gather(summed.astype(jnp.bfloat16), 'pb', axis=0, tiled=True)]
    dot_general x2 -> x0, matrix products: 30.4 us -> none  [the longest x1 22.5 us: tile_product(): lax.dot_general(portion, train_tile, (((1,), (1,)), ((), ())), preferred_...]
    mul x1 -> x2, other arithmetic: 0.01 us -> 13 us  [the longest x1 12.3 us: on_device(): scaled.reshape(select.shape[0], BLK, select.shape[1], BLK)]
    all_to_all x1 -> x0, local copies, waits for them, and re-layouts: 11.4 us -> none  [on_device(): lax.all_to_all(train_features, 'pb', split_axis=0, concat_axis=1, tiled=T...]
    all_to_all x1 -> x0, starting transfers between devices: 4.96 us -> none  [on_device(): lax.all_to_all(train_features, 'pb', split_axis=0, concat_axis=1, tiled=T...]
  transfers between devices with their start and end apart: 4 -> 0, of which waited for: 3 -> 0; matrix products, arithmetic and copies ran while one was open for 3% -> 0% of each run, Pallas kernels for 0% -> 0%
where the time goes in v1:
time: 332 us
  Pallas kernels  314 us (95%)
  other arithmetic  13.7 us (4%)
  local copies, waits for them, and re-layouts  3.9 us (1%)
    pallas_call x1, Pallas kernels, on_device(): pl.pallas_call(functools.partial(kernel, ex_count, pb_count), out_shape=j...  314 us
    mul x1, other arithmetic, on_device(): scaled.reshape(select.shape[0], BLK, select.shape[1], BLK)  12.3 us

profile of v1, /device:TPU:0, one launch (start us, length us, event | category | flops | bytes accessed | tf_op | source)
XLA Modules:
  0.0 331.9 jit_solution(3875143674098092120)
XLA Ops:
  0.0 0.7 broadcast_multiply_fusion
  0.7 0.7 convert_element_type.3
  1.4 0.1 copy.6
  1.5 3.8 %mul.29 = f32[16,128,8,128]{3,2,1,0:T(8,128)} broadcast(f32[16,8]{1,0:T(8,128)S(1)} %copy.6), dimensions={0,2} | broadcast | bytes 8389120 | tf_op jit(solution)/shard_map/mul | solution.py:248
  5.3 314.3 %shard_map.55 = f32[2048,1024]{1,0:T(8,128)} custom-call(bf16[8192,512]{1,0:T(8,128)(2,1)} %train.1, bf16[512,512]{1,0:T(8,128)(2,1)} %query.1, bf16[512,4096]{1,0:T(8,128)(2,1)} %pre.1), custom_call_target="tpu_custom_call" | custom-call | tf_op jit(solution)/shard_map/pallas_call | solution.py:227
  319.6 12.3 %bitcast_multiply_fusion = f32[2048,1024]{1,0:T(8,128)} fusion(f32[256,8,8,128]{3,2,1,0:T(8,128)} %bitcast.4, f32[2048,1024]{1,0:T(8,128)} %shard_map.55, f32[1024]{0:T(1024)S(1)} %broadcast_multiply_fusion), kind=kLoop, calls=%fused_computation | loop fusion | flops 4194304 | bytes 25169920 | tf_op jit(solution)/shard_map/mul | solution.py:248

commit v2 on v1

--- a/solution.py
+++ b/solution.py
@@ -9,6 +9,7 @@
 
 BLK = 128
 ROW_TILE = 512
+CHUNKS = 4
 
 
 def flip(index, mask):
@@ -36,7 +37,7 @@
     return 8 * pb_count + 8 * ex_count
 
 
-def kernel(ex_count, pb_count, train, query, pre, out, q_all, p_all, c_all, t_all, c_sum, send_sem, recv_sem, local_sem):
+def kernel(ex_count, pb_count, train, query, pre, factor, out, q_all, p_all, c_all, t_all, c_sum, send_sem, recv_sem, local_sem):
     e, p = lax.axis_index("ex"), lax.axis_index("pb")
     core, line = p % 2, p // 2
     rows, width = query.shape
@@ -108,17 +109,14 @@
         own(pre_part(p), p_all.at[p, e], 1),
         own(train.at[pl.ds(pl.multiple_of(p * t_rows, t_rows), t_rows), :], t_all.at[p], 2),
     ]
-    far = list(range(pb_count - 1, top - 1, -1))
-    near = list(range(top - 1, 0, -1))
-    train_copies = {}
-    early = far[: len(far) // 2]
-    for mask in early[:1]:
-        train_copies[mask] = start_train(mask)
+    train_copies = {1: start_train(1)}
     local[0].wait()
     local[1].wait()
     arrive(pending_q)
     pending_q = start_query(query_stages[1])
     arrive(pending_p)
+    for mask in [pb_count - 1]:
+        train_copies[mask] = start_train(mask)
 
     half = pb_count // 2
     ex_orders = [ex_bits, ex_bits[1:] + ex_bits[:1]]
@@ -142,52 +140,73 @@
         pending_q = start_query(query_stages[q_next])
         q_next += 1
     arrive(pending_q)
-    for mask in early[1:]:
+
+    across = {"pb": flip(p, 1)}
+    chunk_rows = rows // CHUNKS
+
+    def chunk_part(chunk, ex_mask, where):
+        first = flip(e, ex_mask) * rows + chunk * chunk_rows
+        return c_all.at[core, where, pl.ds(pl.multiple_of(first, chunk_rows), chunk_rows), :]
+
+    line_stages = gather_stages([bit // 2 for bit in pb_bits[:0:-1]])
+
+    def start_line(chunk, stage):
+        bit, held = stage
+        copies = []
+        for mask in held:
+            part = chunk_part(chunk, 0, flip(line, mask))
+            copies.append(send(part, part, {"pb": flip(p, 2 * bit)}))
+        return copies
+
+    def start_ex(chunk, stage):
+        bit, held = stage
+        copies = []
+        for mask in held:
+            part = chunk_part(chunk, mask, slice(None))
+            copies.append(send(part, part, {"ex": flip(e, bit)}))
+        return copies
+
+    handed = []
+    pending = {}
+    for chunk in range(CHUNKS):
+        c_sum[...] = jnp.zeros_like(c_sum)
+
+        def accumulate(block, carry, chunk=chunk):
+            c_sum[...] += jnp.dot(
+                q_all[block, chunk * chunk_rows : (chunk + 1) * chunk_rows, :],
+                p_all[block].reshape(ex_count * share, width),
+                preferred_element_type=jnp.float32,
+            )
+            return carry
+
+        lax.fori_loop(0, pb_count, accumulate, 0)
+        first = pl.multiple_of(e * rows + chunk * chunk_rows, chunk_rows)
+        c_all[core, line, pl.ds(first, chunk_rows), :] = c_sum[...].astype(jnp.bfloat16)
+        pending[chunk] = start_line(chunk, line_stages[0])
+    for stage in line_stages[1:]:
+        for chunk in range(CHUNKS):
+            arrive(pending[chunk])
+            pending[chunk] = start_line(chunk, stage)
+    for mask in [pb_count - 2]:
         train_copies[mask] = start_train(mask)
-
-    c_sum[...] = jnp.zeros_like(c_sum)
-
-    def accumulate(block, carry):
-        c_sum[...] += jnp.dot(
-            q_all[block],
-            p_all[block].reshape(ex_count * share, width),
-            preferred_element_type=jnp.float32,
-        )
-        return carry
-
-    lax.fori_loop(0, pb_count, accumulate, 0)
-    own_rows = pl.ds(pl.multiple_of(e * rows, rows), rows)
-    c_all[core, line, own_rows, :] = c_sum[...].astype(jnp.bfloat16)
-
-    across = {"pb": flip(p, 1)}
-    handed = []
-    for bit, held in gather_stages([bit // 2 for bit in pb_bits[:0:-1]]):
-        pending = []
-        for mask in held:
-            part = c_all.at[core, flip(line, mask), own_rows, :]
-            pending.append(send(part, part, {"pb": flip(p, 2 * bit)}))
-        arrive(pending)
-    for mask in far:
+    for chunk in range(CHUNKS):
+        arrive(pending[chunk])
+        pending[chunk] = start_ex(chunk, ex_stages[chunk % 2][0])
+        part = chunk_part(chunk, 0, slice(None))
+        handed.append(send(part, part, across))
+    for mask in range(pb_count - 1, 0, -1):
         if mask not in train_copies:
             train_copies[mask] = start_train(mask)
-    part = c_all.at[core, :, own_rows, :]
-    handed.append(send(part, part, across))
-    for mask in near:
-        train_copies[mask] = start_train(mask)
-    side_rows = rows // 2
     for step in range(len(ex_bits)):
-        pending, arriving = [], []
-        for side in range(2):
-            bit, held = ex_stages[side][step]
+        for chunk in range(CHUNKS):
+            bit, held = ex_stages[chunk % 2][step]
+            arrived = pending[chunk]
+            arrive(arrived)
+            if step + 1 < len(ex_bits):
+                pending[chunk] = start_ex(chunk, ex_stages[chunk % 2][step + 1])
             for mask in held:
-                first = flip(e, mask) * rows + side * side_rows
-                part = c_all.at[core, :, pl.ds(pl.multiple_of(first, side_rows), side_rows), :]
-                pending.append(send(part, part, {"ex": flip(e, bit)}))
-                first = flip(e, mask ^ bit) * rows + side * side_rows
-                arriving.append(c_all.at[core, :, pl.ds(pl.multiple_of(first, side_rows), side_rows), :])
-        for copy, part in zip(pending, arriving):
-            copy.wait_recv()
-            handed.append(send(part, part, across))
+                part = chunk_part(chunk, mask ^ bit, slice(None))
+                handed.append(send(part, part, across))
     arrive(handed)
 
     for mask in range(pb_count):
@@ -207,8 +226,13 @@
             )
             if mask == 0:
                 out[at, :] = product
+            elif mask < pb_count - 1:
+                out[at, :] += product
             else:
-                out[at, :] += product
+                for part in range(ROW_TILE // BLK):
+                    here = pl.ds(pl.multiple_of(step * ROW_TILE + part * BLK, BLK), BLK)
+                    total = out[here, :] + product[part * BLK : (part + 1) * BLK, :]
+                    out[here, :] = total * factor[pl.ds(step * (ROW_TILE // BLK) + part, 1), :]
             return carry
 
         lax.fori_loop(0, out.shape[0] // ROW_TILE, tile, 0)
@@ -224,17 +248,19 @@
     share = precond.shape[0] // ex_count
     feature_width = width * pb_count
     copies = copy_count(ex_count, pb_count)
-    raw = pl.pallas_call(
+    scale = example_weight * feature_width ** (-0.5)
+    factor = jnp.repeat(select.astype(jnp.float32), BLK, axis=1) * scale[None, :]
+    return pl.pallas_call(
         functools.partial(kernel, ex_count, pb_count),
         out_shape=jax.ShapeDtypeStruct((queries, t_rows), jnp.float32),
-        in_specs=[pl.BlockSpec(memory_space=pl.ANY)] * 3,
+        in_specs=[pl.BlockSpec(memory_space=pl.ANY)] * 3 + [pl.BlockSpec(memory_space=pltpu.VMEM)],
         out_specs=pl.BlockSpec(memory_space=pltpu.VMEM),
         scratch_shapes=[
             pltpu.VMEM((pb_count, rows, width), jnp.bfloat16),
             pltpu.VMEM((pb_count, ex_count, share, width), jnp.bfloat16),
             pltpu.VMEM((2, pb_count // 2, queries, width), jnp.bfloat16),
             pltpu.VMEM((pb_count, t_rows, width), jnp.bfloat16),
-            pltpu.VMEM((rows, width), jnp.float32),
+            pltpu.VMEM((rows // CHUNKS, width), jnp.float32),
             pltpu.SemaphoreType.DMA((copies,)),
             pltpu.SemaphoreType.DMA((copies,)),
             pltpu.SemaphoreType.DMA((3,)),
@@ -242,11 +268,7 @@
         compiler_params=pltpu.CompilerParams(
             collective_id=0, has_side_effects=True, vmem_limit_bytes=56 * 1024 * 1024
         ),
-    )(train_features, query_features, precond)
-    scaled = raw * feature_width ** (-0.5) * example_weight[None, :]
-    keep_mask = select.astype(jnp.float32)
-    masked = scaled.reshape(select.shape[0], BLK, select.shape[1], BLK) * keep_mask[:, None, :, None]
-    return masked.reshape(raw.shape)
+    )(train_features, query_features, precond, factor)
 
 
 def solution(mesh):

time: 332 us -> 283 us (0.85)
  Pallas kernels: 314 us -> 272 us
  other arithmetic: 13.7 us -> 2.03 us
  local copies, waits for them, and re-layouts: 3.9 us -> 8.59 us
    pallas_call x1, Pallas kernels: 314 us -> 272 us  [on_device(): pl.pallas_call(functools.partial(kernel, ex_count, pb_count), out_shape=j...]
    mul x2, other arithmetic: 13 us -> 1.34 us  [the longest x1 0.69 us: on_device(): scale = example_weight * feature_width ** (-0.5)]
    unnamed x0 -> x1, local copies, waits for them, and re-layouts: none -> 8.44 us
    mul x1 -> x0, local copies, waits for them, and re-layouts: 3.83 us -> none  [on_device(): scaled.reshape(select.shape[0], BLK, select.shape[1], BLK)]
where the time goes in v2:
time: 283 us
  Pallas kernels  272 us (96%)
  local copies, waits for them, and re-layouts  8.59 us (3%)
    pallas_call x1, Pallas kernels, on_device(): pl.pallas_call(functools.partial(kernel, ex_count, pb_count), out_shape=j...  272 us
    unnamed x1, local copies, waits for them, and re-layouts  8.44 us

profile of v2, /device:TPU:0, one launch (start us, length us, event | category | flops | bytes accessed | tf_op | source)
XLA Modules:
  0.0 282.9 jit_solution(7011867018257321275)
XLA Ops:
  0.0 0.7 broadcast_multiply_fusion
  0.7 0.7 convert_element_type.3
  1.4 0.1 copy.6
  1.5 0.1 broadcast_in_dim.4
  1.5 0.7 bitcast_multiply_fusion.factor
  2.2 272.2 %shard_map.55 = f32[2048,1024]{1,0:T(8,128)} custom-call(bf16[8192,512]{1,0:T(8,128)(2,1)} %train.1, bf16[512,512]{1,0:T(8,128)(2,1)} %query.1, bf16[512,4096]{1,0:T(8,128)(2,1)} %pre.1, f32[16,1024]{1,0:T(8,128)} %bitcast_multiply_fusion.factor), custom_call_target="tpu_custom_call" | custom-call | tf_op jit(solution)/shard_map/pallas_call | solution.py:253
  274.4 8.4 %copy.10 = f32[2048,1024]{1,0:T(8,128)} copy(f32[2048,1024]{1,0:T(8,128)} %shard_map.55) | data formatting | bytes 16777216

commit v3 on v2

--- a/solution.py
+++ b/solution.py
@@ -194,9 +194,8 @@
         pending[chunk] = start_ex(chunk, ex_stages[chunk % 2][0])
         part = chunk_part(chunk, 0, slice(None))
         handed.append(send(part, part, across))
-    for mask in range(pb_count - 1, 0, -1):
-        if mask not in train_copies:
-            train_copies[mask] = start_train(mask)
+    for mask in [*range(top - 1, 1, -1), *range(pb_count - 3, top, -1)]:
+        train_copies[mask] = start_train(mask)
     for step in range(len(ex_bits)):
         for chunk in range(CHUNKS):
             bit, held = ex_stages[chunk % 2][step]
@@ -207,35 +206,45 @@
             for mask in held:
                 part = chunk_part(chunk, mask ^ bit, slice(None))
                 handed.append(send(part, part, across))
+    train_copies[top] = start_train(top)
     arrive(handed)
 
-    for mask in range(pb_count):
-        if mask == 0:
-            local[2].wait()
-        else:
-            train_copies[mask].wait_recv()
-        block = flip(p, mask)
-
-        def tile(step, carry, block=block, mask=mask):
+    def product(block, at):
+        return lax.dot_general(
+            c_all[block % 2, block // 2, at, :],
+            t_all[block],
+            (((1,), (1,)), ((), ())),
+            preferred_element_type=jnp.float32,
+        )
+
+    def scores(masks, opening, closing):
+        blocks = [flip(p, mask) for mask in masks]
+
+        def tile(step, carry):
             at = pl.ds(pl.multiple_of(step * ROW_TILE, ROW_TILE), ROW_TILE)
-            product = lax.dot_general(
-                c_all[block % 2, block // 2, at, :],
-                t_all[block],
-                (((1,), (1,)), ((), ())),
-                preferred_element_type=jnp.float32,
-            )
-            if mask == 0:
-                out[at, :] = product
-            elif mask < pb_count - 1:
-                out[at, :] += product
+            total = product(blocks[0], at)
+            for block in blocks[1:]:
+                total += product(block, at)
+            if opening:
+                out[at, :] = total
+            elif not closing:
+                out[at, :] += total
             else:
                 for part in range(ROW_TILE // BLK):
                     here = pl.ds(pl.multiple_of(step * ROW_TILE + part * BLK, BLK), BLK)
-                    total = out[here, :] + product[part * BLK : (part + 1) * BLK, :]
-                    out[here, :] = total * factor[pl.ds(step * (ROW_TILE // BLK) + part, 1), :]
+                    block_sum = out[here, :] + total[part * BLK : (part + 1) * BLK, :]
+                    out[here, :] = block_sum * factor[pl.ds(step * (ROW_TILE // BLK) + part, 1), :]
             return carry
 
         lax.fori_loop(0, out.shape[0] // ROW_TILE, tile, 0)
+
+    groups = [[*range(top), pb_count - 1], *([mask] for mask in range(pb_count - 2, top - 1, -1))]
+    local[2].wait()
+    for group in groups:
+        for mask in group:
+            if mask > 0:
+                train_copies[mask].wait_recv()
+        scores(group, group is groups[0], group is groups[-1])
 
     for copy in used:
         copy.wait_send()

time: 283 us -> 279 us (0.986)
  Pallas kernels: 272 us -> 268 us
    pallas_call x1, Pallas kernels: 272 us -> 268 us  [on_device(): pl.pallas_call(functools.partial(kernel, ex_count, pb_count), out_shape=j...]
where the time goes in v3:
time: 279 us; the launch traced here: 278 us
  Pallas kernels  268 us (96%)
  local copies, waits for them, and re-layouts  8.59 us (3%)
    pallas_call x1, Pallas kernels, on_device(): pl.pallas_call(functools.partial(kernel, ex_count, pb_count), out_shape=j...  268 us
    unnamed x1, local copies, waits for them, and re-layouts  8.44 us

profile of v3, /device:TPU:0, one launch (start us, length us, event | category | flops | bytes accessed | tf_op | source)
XLA Modules:
  0.0 278.3 jit_solution(6876104768504811632)
XLA Ops:
  0.0 0.7 broadcast_multiply_fusion
  0.7 0.7 convert_element_type.3
  1.4 0.1 copy.6
  1.5 0.1 broadcast_in_dim.4
  1.5 0.7 bitcast_multiply_fusion.factor
  2.2 267.7 %shard_map.55 = f32[2048,1024]{1,0:T(8,128)} custom-call(bf16[8192,512]{1,0:T(8,128)(2,1)} %train.1, bf16[512,512]{1,0:T(8,128)(2,1)} %query.1, bf16[512,4096]{1,0:T(8,128)(2,1)} %pre.1, f32[16,1024]{1,0:T(8,128)} %bitcast_multiply_fusion.factor), custom_call_target="tpu_custom_call" | custom-call | tf_op jit(solution)/shard_map/pallas_call | solution.py:262
  269.9 8.4 %copy.10 = f32[2048,1024]{1,0:T(8,128)} copy(f32[2048,1024]{1,0:T(8,128)} %shard_map.55) | data formatting | bytes 16777216
